TPU v7x, 512 devices: a whole 4x4x16 slice. The times are simulated.
512 devices in a mesh: tm: 8 (over x, y_lo), height: 64 (over z, y_hi, core).
Axes of the slice: x: 4, y: 4 (y_hi: 2, y_lo: 2; y = y_hi * 2 + y_lo), z: 16, core: 2. Of those that a mesh axis runs over, the one named last changes fastest.
Arguments:
- query_raw: bfloat16 [16, 64, 80, 1536], P('tm', 'height'), may hold values from -40 to 40
- key_raw: bfloat16 [16, 64, 80, 1536], P('tm', 'height'), may hold values from -40 to 40
- values: bfloat16 [16, 64, 80, 1536], P('tm', 'height'), may hold values from -6 to 6
- out_grad: bfloat16 [16, 64, 80, 1536], P('tm', 'height'), may hold values from -6 to 6
- query_gain: float32 [128], replicated, may hold values from 0.5 to 1.5
- key_gain: float32 [128], replicated, may hold values from 0.5 to 1.5
- window: int32 [12, 3], replicated, may hold values from 0 to 2, as said below
Outputs:
- query_grad: bfloat16 [16, 64, 80, 1536], P('tm', 'height')
- key_grad: bfloat16 [16, 64, 80, 1536], P('tm', 'height')
- value_grad: bfloat16 [16, 64, 80, 1536], P('tm', 'height')
- gain_grad: float32 [2, 128], P(None, 'height')
Inputs may be any that keep to these rules, and one draw needn't show every extreme that they name: `window`: columns 0 and 1 hold 0 or 1 and column 2 holds 0 to 2; some head has reach (1, 1, 2) and some head (0, 0, 0).
All inputs are finite; a program needn't handle non-finite values.
Results may differ from a plain program's by a relative error of at most 0.008.
Values may be sent and summed in bfloat16 or wider, within the bound.
No kernel may reach another device: no remote copies, remote signals or barrier semaphores. Data moves between devices by JAX's collectives and lax.ppermute only.
A program may use at most 128 MiB of HBM per device.

v0:
```python
import functools

import jax
import jax.numpy as jnp
from jax import lax
from jax.experimental import pallas as pl
from jax.experimental.pallas import tpu as pltpu
from jax.sharding import PartitionSpec as P

TILE_W = 8
EPSILON = 1e-06
HEAD_DIM = 128
LOG2E = 1.4426950408889634
BLOCKED = 1000.0
LANES = 128
BOTH = ("tm", "height")
SIZES = [(6, 6, 4), (8, 8, 6), (10, 10, 8)]
GROUP = 3
VMEM_BYTES = 56 * 1024 * 1024


def rms_inverse(full_rows):
    return lax.rsqrt(jnp.mean(full_rows * full_rows, axis=-1, keepdims=True) + EPSILON)


def norm_backward(grad_rows, unit_rows, inverse, gain_row):
    scaled = grad_rows * gain_row
    return inverse * (scaled - unit_rows * jnp.mean(unit_rows * scaled, axis=-1, keepdims=True))


def whole(memory_space=pltpu.VMEM):
    return pl.BlockSpec(memory_space=memory_space)


def params():
    return pltpu.CompilerParams(vmem_limit_bytes=VMEM_BYTES)


def head_lanes(g):
    return pl.ds(pl.multiple_of(g * LANES, LANES), LANES)


def pack_kernel(
    window_ref, key_ref, value_ref, gain_ref,
    slots_ref, own_ref, row_ref, first_ref, last_ref, corner_first_ref, corner_last_ref,
):
    frames, width, channels = key_ref.shape
    gain_row = gain_ref[...]
    heads = channels // LANES
    edges = ((first_ref, corner_first_ref), (last_ref, corner_last_ref))

    def one_head(g, counts):
        lanes = head_lanes(g)
        row_on, frame_on = window_ref[g, 1], window_ref[g, 0]
        counts = tuple(c + on for c, on in zip(counts, (row_on, frame_on, row_on * frame_on)))
        slots = [jnp.maximum(c - 1, 0) for c in counts]
        for kind in range(3):
            slots_ref[kind, g] = slots[kind]
        slots_ref[3, jnp.where(row_on * frame_on == 1, slots[2], heads - 1 - (g - counts[2]))] = g
        pairs = []
        for f in range(frames):
            full_rows = key_ref[f, :, lanes].astype(jnp.float32)
            pairs.append(
                ((full_rows * rms_inverse(full_rows) * gain_row).astype(jnp.bfloat16), value_ref[f, :, lanes])
            )
            for c in range(2):
                own_ref[f, c, :, lanes] = pairs[f][c]

        @pl.when(row_on == 1)
        def _():
            for f in range(frames):
                for c in range(2):
                    row_ref[slots[0], f, c] = pairs[f][c]

        @pl.when(frame_on == 1)
        def _():
            for f in range(frames):
                for c in range(2):
                    edges[f][0][slots[1], c] = pairs[f][c]

        @pl.when(row_on * frame_on == 1)
        def _():
            for f in range(frames):
                for c in range(2):
                    edges[f][1][slots[2], c] = pairs[f][c]

        return counts

    zero = jnp.int32(0)
    counts = lax.fori_loop(0, heads, one_head, (zero, zero, zero))
    slots_ref[4, 0] = counts[2]


def pack(window, key_raw, values, key_gain, sizes):
    frames, width, channels = key_raw.shape
    kinds = jax.ShapeDtypeStruct
    low = jnp.bfloat16
    shapes = [(frames, 2, width, channels), (sizes[0], frames, 2, width, LANES)]
    shapes += [(sizes[1], 2, width, LANES)] * 2 + [(sizes[2], 2, width, LANES)] * 2
    return pl.pallas_call(
        pack_kernel,
        in_specs=[whole(pltpu.SMEM)] + [whole()] * 3,
        out_specs=[whole(pltpu.SMEM)] + [whole()] * 6,
        out_shape=[kinds((5, channels // LANES), jnp.int32)] + [kinds(shape, low) for shape in shapes],
        compiler_params=params(),
        name="pack_keys_values",
    )(window, key_raw, values, key_gain)


def matmul(a, b, dims):
    return lax.dot_general(a, b, (dims, ((), ())), preferred_element_type=jnp.float32)


def attend_kernel(
    window_ref, slots_ref, query_ref, grad_ref, own_ref, chip_ref, off_ref,
    prev_ref, next_ref, chip_prev_ref, chip_next_ref, off_prev_ref, off_next_ref,
    q_gain_ref, k_gain_ref,
    query_grad_ref, own_out, chip_out, off_out, prev_out, next_out, gain_out,
    key_buf, value_buf, key_sum, value_sum, gap_ref,
):
    frames, width, _ = query_ref.shape
    heads = window_ref.shape[0]
    scale = LANES ** (-0.5)
    row_slots = chip_ref.shape[0]
    both = range(frames)
    key_buf[...] = jnp.zeros_like(key_buf)
    value_buf[...] = jnp.zeros_like(value_buf)
    gain_out[...] = jnp.zeros_like(gain_out)
    queries, keys = gap_ref.shape
    q_tile = lax.broadcasted_iota(jnp.int32, (queries, LANES), 0) // TILE_W
    for first in range(0, keys, LANES):
        k_ids = first + lax.broadcasted_iota(jnp.int32, (8, LANES), 1)
        k_tile = (k_ids % width // TILE_W)[0:1]
        gap_ref[:, first : first + LANES] = jnp.abs(q_tile - k_tile).astype(jnp.float32)
    gain_row = q_gain_ref[...]
    full, part = span_sizes(width)
    t, h = lax.axis_index("tm"), lax.axis_index("height")
    has_off = jnp.logical_and(h > 0, h < lax.axis_size("height") - 1).astype(jnp.int32)
    has_prev = (t > 0).astype(jnp.int32)
    has_next = (t < lax.axis_size("tm") - 1).astype(jnp.int32)

    def each_block(g, do):
        frame_reach, row_reach = window_ref[g, 0], window_ref[g, 1]
        row_count = 1 + 2 * row_reach
        row_slot, frame_slot, corner_slot = slots_ref[0, g], slots_ref[1, g], slots_ref[2, g]
        lanes = head_lanes(g)

        def place(r, e):
            return pl.ds(pl.multiple_of((e * row_count + r) * width, 16), width)

        for f in both:
            do(place(0, f + 1), own_ref.at[f, :, :, lanes], own_out.at[g, f])

        @pl.when(frame_reach == 1)
        def _():
            do(place(0, 0), prev_ref.at[frame_slot], prev_out.at[frame_slot])
            do(place(0, frames + 1), next_ref.at[frame_slot], next_out.at[frame_slot])

        @pl.when(row_reach == 1)
        def _():
            for f in both:
                do(place(1, f + 1), chip_ref.at[row_slot, f], chip_out.at[row_slot, f])
                do(place(2, f + 1), off_ref.at[row_slot, f], off_out.at[row_slot, f])

        @pl.when(frame_reach * row_reach == 1)
        def _():
            last = row_slots + corner_slot
            do(place(1, 0), chip_prev_ref.at[frame_slot], chip_out.at[last, 0])
            do(place(1, frames + 1), chip_next_ref.at[frame_slot], chip_out.at[last, 1])
            do(place(2, 0), off_prev_ref.at[corner_slot], off_out.at[last, 0])
            do(place(2, frames + 1), off_next_ref.at[corner_slot], off_out.at[last, 1])

    def work(group, counted, keys):
        for n, g in enumerate(group):

            def load(place, source, _, n=n):
                key_buf[n, place] = source[0]
                value_buf[n, place] = source[1]

            each_block(g, load)
        gap = gap_ref[:, 0:keys]
        k_ids = lax.broadcasted_iota(jnp.int32, (1, keys), 1)
        chains = [(n, f) for n in range(len(group)) for f in both]
        spans, inside, unit, inverse, queries, grads = {}, {}, {}, {}, {}, {}
        for n, g in enumerate(group):
            frame_reach, row_reach = window_ref[g, 0], window_ref[g, 1]
            tile_reach = window_ref[g, 2].astype(jnp.float32)
            lanes = head_lanes(g)
            per_frame = (1 + 2 * row_reach) * width
            frame = jnp.zeros_like(k_ids)
            for m in range(1, 4):
                frame += (k_ids >= m * per_frame).astype(jnp.int32)
            rest = k_ids - frame * per_frame
            off_row = jnp.logical_and(rest >= 2 * width, has_off == 0)
            for f in both:
                begin = f + 1 - frame_reach
                spans[n, f] = pl.ds(pl.multiple_of(begin * per_frame, 16), keys)
                shut = jnp.logical_or(frame > 2 * frame_reach, off_row)
                shut = jnp.logical_or(shut, jnp.logical_and(begin + frame == 0, has_prev == 0))
                shut = jnp.logical_or(shut, jnp.logical_and(begin + frame == frames + 1, has_next == 0))
                inside[n, f] = gap + jnp.where(shut, BLOCKED, 0.0) <= tile_reach
                full_rows = query_ref[f, :, lanes].astype(jnp.float32)
                inverse[n, f] = rms_inverse(full_rows)
                unit[n, f] = full_rows * inverse[n, f]
                queries[n, f] = (unit[n, f] * gain_row).astype(jnp.bfloat16)
                grads[n, f] = grad_ref[f, :, lanes]
            key_sum[n, pl.ds(pl.multiple_of((1 - frame_reach) * per_frame + keys, 16), 3 * width)] = jnp.zeros(
                (3 * width, LANES), jnp.float32
            )
            value_sum[n, pl.ds(pl.multiple_of((1 - frame_reach) * per_frame + keys, 16), 3 * width)] = jnp.zeros(
                (3 * width, LANES), jnp.float32
            )
        scores = {i: matmul(queries[i], key_buf[i[0], spans[i]], ((1,), (1,))) for i in chains}
        prob_back = {i: matmul(grads[i], value_buf[i[0], spans[i]], ((1,), (1,))) for i in chains}
        weight = {i: jnp.where(inside[i], jnp.exp2(scores[i] * (scale * LOG2E)), 0.0) for i in chains}
        over = {i: 1.0 / jnp.sum(weight[i], axis=-1, keepdims=True) for i in chains}
        delta = {i: jnp.sum(weight[i] * prob_back[i], axis=-1, keepdims=True) * over[i] for i in chains}
        prob = {i: weight[i] * over[i] for i in chains}
        score_back = {i: (prob[i] * ((prob_back[i] - delta[i]) * scale)).astype(jnp.bfloat16) for i in chains}
        query_back = {i: matmul(score_back[i], key_buf[i[0], spans[i]], ((1,), (0,))) for i in chains}
        key_back = {i: matmul(score_back[i], queries[i], ((0,), (0,))) for i in chains}
        value_back = {i: matmul(prob[i].astype(jnp.bfloat16), grads[i], ((0,), (0,))) for i in chains}
        for i in chains:
            n, f = i
            if f == 0:
                key_sum[n, spans[i]] = key_back[i]
                value_sum[n, spans[i]] = value_back[i]
            else:
                key_sum[n, spans[i]] += key_back[i]
                value_sum[n, spans[i]] += value_back[i]
            result = norm_backward(query_back[i], unit[i], inverse[i], gain_row)
            query_grad_ref[f, :, head_lanes(group[n])] = result.astype(query_grad_ref.dtype)
        first = jnp.zeros((1, LANES), jnp.float32)
        second = first
        for i in chains:
            once = counted[i[0]]
            first += once * jnp.sum(query_back[i] * unit[i], axis=0, keepdims=True)
            second += once * jnp.sum(query_back[i] * queries[i].astype(jnp.float32), axis=0, keepdims=True)
        gain_out[0:1] += first
        gain_out[1:2] += second / k_gain_ref[...]
        for n, g in enumerate(group):

            def store(place, _, out, n=n):
                out[0] = key_sum[n, place].astype(out.dtype)
                out[1] = value_sum[n, place].astype(out.dtype)

            each_block(g, store)

    wide = slots_ref[4, 0]

    def one_wide(i, carry):
        work([slots_ref[3, i]], [1.0], full)
        return carry

    def narrow_group(j, carry):
        places = [wide + GROUP * j + n for n in range(GROUP)]
        group = [slots_ref[3, jnp.minimum(place, heads - 1)] for place in places]
        work(group, [(place < heads).astype(jnp.float32) for place in places], part)
        return carry

    lax.fori_loop(0, wide, one_wide, 0)
    lax.fori_loop(0, (heads - wide + GROUP - 1) // GROUP, narrow_group, 0)


def span_sizes(width):
    return tuple(-(-blocks * width // LANES) * LANES for blocks in (9, 3))


def attend(window, slots, query_raw, out_grad, own, chip, off, edges, corners, query_gain, key_gain):
    frames, width, channels = query_raw.shape
    heads = channels // LANES
    kinds = jax.ShapeDtypeStruct
    sent_shape = (chip.shape[0] + corners[0].shape[0], frames, 2, width, LANES)
    edge_shape = edges[0].shape
    most = 3 * width + span_sizes(width)[0]
    return pl.pallas_call(
        attend_kernel,
        in_specs=[whole(pltpu.SMEM)] * 2 + [whole()] * 13,
        out_specs=[whole()] * 7,
        out_shape=[
            kinds(query_raw.shape, jnp.bfloat16),
            kinds((heads, frames, 2, width, LANES), jnp.float32),
            kinds(sent_shape, jnp.bfloat16),
            kinds(sent_shape, jnp.bfloat16),
            kinds(edge_shape, jnp.float32),
            kinds(edge_shape, jnp.float32),
            kinds((2, LANES), jnp.float32),
        ],
        scratch_shapes=[
            pltpu.VMEM((GROUP, most, LANES), jnp.bfloat16),
            pltpu.VMEM((GROUP, most, LANES), jnp.bfloat16),
            pltpu.VMEM((GROUP, most, LANES), jnp.float32),
            pltpu.VMEM((GROUP, most, LANES), jnp.float32),
            pltpu.VMEM((width, span_sizes(width)[0]), jnp.float32),
        ],
        compiler_params=params(),
        name="attend",
    )(window, slots, query_raw, out_grad, own, chip, off, *edges, *corners, query_gain, key_gain)


def relay_kernel(row_slots, window_ref, slots_ref, prev_ref, next_ref, chip_ref, off_ref, prev_out, next_out):

    def one_head(g, carry):
        row_on, frame_on = window_ref[g, 1], window_ref[g, 0]
        corner_slot, frame_slot = row_slots + slots_ref[2, g], slots_ref[1, g]

        @pl.when(jnp.logical_and(frame_on == 1, row_on == 0))
        def _():
            for kept, out in ((prev_ref, prev_out), (next_ref, next_out)):
                out[frame_slot] = kept[frame_slot].astype(out.dtype)

        @pl.when(jnp.logical_and(frame_on == 1, row_on == 1))
        def _():
            for kept, out, e in ((prev_ref, prev_out, 0), (next_ref, next_out, 1)):
                terms = kept[frame_slot] + chip_ref[corner_slot, e].astype(jnp.float32)
                out[frame_slot] = (terms + off_ref[corner_slot, e].astype(jnp.float32)).astype(out.dtype)

        return carry

    lax.fori_loop(0, window_ref.shape[0], one_head, 0)


def relay(window, slots, kept, chip, off, row_slots):
    return pl.pallas_call(
        functools.partial(relay_kernel, row_slots),
        in_specs=[whole(pltpu.SMEM)] * 2 + [whole()] * 4,
        out_specs=[whole()] * 2,
        out_shape=[jax.ShapeDtypeStruct(kept[0].shape, jnp.bfloat16)] * 2,
        compiler_params=params(),
        name="add_corner_terms",
    )(window, slots, *kept, chip, off)


def finish_kernel(
    window_ref, slots_ref, key_ref, own_ref, chip_ref, off_ref, first_ref, last_ref, gain_ref,
    key_grad_ref, value_grad_ref,
):
    frames = key_ref.shape[0]
    gain_row = gain_ref[...]
    edges = (first_ref, last_ref)

    def one_head(g, carry):
        lanes = head_lanes(g)
        row_on, frame_on = window_ref[g, 1] == 1, window_ref[g, 0] == 1
        row_slot, frame_slot = slots_ref[0, g], slots_ref[1, g]
        for f in range(frames):
            sums = []
            for c in range(2):
                rows = chip_ref[row_slot, f, c].astype(jnp.float32) + off_ref[row_slot, f, c].astype(jnp.float32)
                edge = edges[f][frame_slot, c].astype(jnp.float32)
                sums.append(own_ref[g, f, c] + jnp.where(row_on, rows, 0.0) + jnp.where(frame_on, edge, 0.0))
            full_rows = key_ref[f, :, lanes].astype(jnp.float32)
            inverse = rms_inverse(full_rows)
            result = norm_backward(sums[0], full_rows * inverse, inverse, gain_row)
            key_grad_ref[f, :, lanes] = result.astype(key_grad_ref.dtype)
            value_grad_ref[f, :, lanes] = sums[1].astype(value_grad_ref.dtype)
        return carry

    lax.fori_loop(0, window_ref.shape[0], one_head, 0, unroll=4)


def finish(window, slots, key_raw, own, chip, off, edges, key_gain):
    frames, width, _ = key_raw.shape
    return pl.pallas_call(
        finish_kernel,
        in_specs=[whole(pltpu.SMEM)] * 2 + [whole()] * 7,
        out_specs=[whole()] * 2,
        out_shape=[jax.ShapeDtypeStruct(key_raw.shape, jnp.bfloat16)] * 2,
        compiler_params=params(),
        name="finish_keys",
    )(window, slots, key_raw, own, chip, off, *edges, key_gain)


def off_chip(h):
    return h + 1 if h % 2 else h - 1


def move(block, frame_step, row_rule):
    frames_size, rows_size = lax.axis_size("tm"), lax.axis_size("height")
    route = []
    for t in range(frames_size):
        for h in range(rows_size):
            to_t, to_h = t + frame_step, row_rule(h)
            if 0 <= to_t < frames_size and 0 <= to_h < rows_size:
                route.append((t * rows_size + h, to_t * rows_size + to_h))
    return lax.ppermute(block, BOTH, route)


def same_row(h):
    return h


def chip_row(h):
    return h ^ 1


def sum_over_rows(part):
    rows_size = lax.axis_size("height")
    per_row = LANES // rows_size
    pieces = part.reshape(2, rows_size, per_row).transpose(1, 0, 2).reshape(rows_size, 2 * per_row)
    return lax.all_to_all(pieces, "height", 0, 0, tiled=True).sum(0, keepdims=True)


def sum_over_frames(mine):
    copies = jnp.broadcast_to(mine, (lax.axis_size("tm"), mine.shape[1]))
    return lax.all_to_all(copies, "tm", 0, 0, tiled=True).sum(0).reshape(2, mine.shape[1] // 2)


def with_sizes(sizes, query_flat, key_flat, value_flat, grad_flat, q_gain, k_gain, window):
    slots, own, rows, first, last, corner_first, corner_last = pack(window, key_flat, value_flat, k_gain, sizes)
    off = move(rows, 0, off_chip)
    prev = move(last, 1, same_row)
    following = move(first, -1, same_row)
    off_prev = move(corner_last, 1, off_chip)
    off_next = move(corner_first, -1, off_chip)
    rows, off_prev, off_next = lax.optimization_barrier((rows, off_prev, off_next))
    chip = move(rows, 0, chip_row)
    chip_prev = move(prev, 0, chip_row)
    chip_next = move(following, 0, chip_row)

    query_grad, own_sum, chip_sum, off_sum, prev_sum, next_sum, gain_part = attend(
        window, slots, query_flat, grad_flat, own, chip, off,
        (prev, following, chip_prev, chip_next), (off_prev, off_next), q_gain, k_gain,
    )

    off_back = move(off_sum, 0, off_chip)
    chip_back = move(chip_sum, 0, chip_row)
    mine = sum_over_rows(gain_part)
    chip_back, off_back, mine = lax.optimization_barrier((chip_back, off_back, mine))
    prev_all, next_all = relay(window, slots, (prev_sum, next_sum), chip_back, off_back, sizes[0])
    last_back = move(prev_all, -1, same_row)
    first_back = move(next_all, 1, same_row)
    gain_grad = sum_over_frames(mine)
    first_back, last_back, gain_grad = lax.optimization_barrier((first_back, last_back, gain_grad))
    key_grad, value_grad = finish(
        window, slots, key_flat, own_sum, chip_back, off_back, (first_back, last_back), k_gain
    )
    return query_grad, key_grad, value_grad, gain_grad


def on_device(query_raw, key_raw, values, out_grad, query_gain, key_gain, window):
    frames, _, width, channels = query_raw.shape
    heads = channels // LANES
    flat = (frames, width, channels)
    row_on, frame_on = window[:, 1], window[:, 0]
    row_count, frame_count, both_count = jnp.sum(row_on), jnp.sum(frame_on), jnp.sum(row_on * frame_on)
    choices = SIZES + [(heads, heads, heads)]
    choice = jnp.int32(0)
    for sizes in SIZES:
        fits = (row_count <= sizes[0]) & (frame_count <= sizes[1]) & (both_count <= sizes[2])
        choice += 1 - fits.astype(jnp.int32)
    args = [x.reshape(flat) for x in (query_raw, key_raw, values, out_grad)]
    outs = lax.switch(
        choice,
        [functools.partial(with_sizes, sizes) for sizes in choices],
        *args, query_gain[None], key_gain[None], window,
    )
    return tuple(x.reshape(query_raw.shape) for x in outs[:3]) + (outs[3],)


def solution(mesh):
    token = P("tm", "height", None, None)
    return jax.shard_map(
        on_device,
        mesh=mesh,
        in_specs=(token, token, token, token, P(), P(), P()),
        out_specs=(token, token, token, P(None, "height")),
        check_vma=False,
    )
```

profile of v0, /device:TPU:3, one launch (start us, length us, event | category | flops | bytes accessed | tf_op | source)
XLA Modules:
  0.0 140.9 jit_solution(3745371910705344935)
XLA Ops:
  0.6 1.4 %multiply_reduce_fusion = (s32[]{:T(128)}, s32[]{:T(128)}, s32[]{:T(128)}) fusion(s32[12,3]{0,1:T(4,128)} %param.17), kind=kLoop, calls=%fused_computation | loop fusion | flops 45 | bytes 108 | tf_op jit(solution)/shard_map/reduce_sum | solution.py:446
  7.9 132.4 %conditional.1 = (bf16[2,80,1536]{2,1,0:T(8,128)(2,1)}, bf16[2,80,1536]{2,1,0:T(8,128)(2,1)}, bf16[2,80,1536]{2,1,0:T(8,128)(2,1)}, f32[2,2]{1,0:T(2,128)S(1)}) conditional(s32[]{:T(128)} %clamp.3, (s32[12,3]{0,1:T(4,128)}, bf16[2,80,1536]{2,1,0:T(8,128)(2,1)}, bf16[2,80,1536]{2,1,0:T(8,128)(2,1)}, ...), branch_computations={%region_3.0_spmd, %region_6.0_spmd, %region_9.0_spmd, %region_12.0... | conditional | flops 280 | bytes 72757984 | solution.py:453
  7.9 1.4 copy.60.window_ref
  9.3 4.3 %pack_keys_values.5 = (s32[5,12]{1,0:T(8,128)}, bf16[2,2,80,1536]{3,2,1,0:T(8,128)(2,1)}, bf16[8,2,2,80,128]{4,3,2,1,0:T(8,128)(2,1)}, bf16[8,2,80,128]{3,2,1,0:...) custom-call(s32[12,3]{1,0:T(8,128)} %copy.60.window_ref, ...), custom_call_target="tpu_custom_call" | custom-call | tf_op jit(solution)/shard_map/cond/branch_1_fun/pack_keys_values/pallas_call | solution.py:100
  13.6 5.2 %collective-permute-start.12 = (bf16[6,2,80,128]{3,2,1,0:T(8,128)(2,1)}, bf16[6,2,80,128]{3,2,1,0:T(8,128)(2,1)S(1)}, u32[]{:S(2)}, u32[]{:S(2)}) collective-permute-start(bf16[6,2,80,128]{3,2,1,0:T(8,128)(2,1)} %get-tuple-element.99), channel_id=1, source_target_pairs={{1,66},{2,65},{3,68},{4,67},{5,70},{6,69},{7,72},{8,71},{9,74},{10... | collective-permute-start | bytes 737288 | tf_op jit(solution)/shard_map/cond/branch_1_fun/ppermute | solution.py:386
  18.8 2.5 %collective-permute-start.13 = (bf16[6,2,80,128]{3,2,1,0:T(8,128)(2,1)}, bf16[6,2,80,128]{3,2,1,0:T(8,128)(2,1)S(1)}, u32[]{:S(2)}, u32[]{:S(2)}) collective-permute-start(bf16[6,2,80,128]{3,2,1,0:T(8,128)(2,1)} %get-tuple-element.100), channel_id=1, source_target_pairs={{65,2},{66,1},{67,4},{68,3},{69,6},{70,5},{71,8},{72,7},{73,10},{7... | collective-permute-start | bytes 737288 | tf_op jit(solution)/shard_map/cond/branch_1_fun/ppermute | solution.py:386
  21.3 2.1 %collective-permute-start.16 = (bf16[8,2,80,128]{3,2,1,0:T(8,128)(2,1)}, bf16[8,2,80,128]{3,2,1,0:T(8,128)(2,1)S(1)}, u32[]{:S(2)}, u32[]{:S(2)}) collective-permute-start(bf16[8,2,80,128]{3,2,1,0:T(8,128)(2,1)} %get-tuple-element.102), channel_id=1, source_target_pairs={{0,64},{1,65},{2,66},{3,67},{4,68},{5,69},{6,70},{7,71},{8,72},{9,... | collective-permute-start | bytes 983048 | tf_op jit(solution)/shard_map/cond/branch_1_fun/ppermute | solution.py:386
  23.5 4.0 %collective-permute-start.17 = (bf16[8,2,80,128]{3,2,1,0:T(8,128)(2,1)}, bf16[8,2,80,128]{3,2,1,0:T(8,128)(2,1)S(1)}, u32[]{:S(2)}, u32[]{:S(2)}) collective-permute-start(bf16[8,2,80,128]{3,2,1,0:T(8,128)(2,1)} %get-tuple-element.103), channel_id=1, source_target_pairs={{64,0},{65,1},{66,2},{67,3},{68,4},{69,5},{70,6},{71,7},{72,8},{73... | collective-permute-start | bytes 983048 | tf_op jit(solution)/shard_map/cond/branch_1_fun/ppermute | solution.py:386
  27.5 4.7 %collective-permute-start.15 = (bf16[8,2,2,80,128]{4,3,2,1,0:T(8,128)(2,1)}, bf16[8,2,2,80,128]{4,3,2,1,0:T(8,128)(2,1)S(1)}, u32[]{:S(2)}, u32[]{:S(2)}) collective-permute-start(bf16[8,2,2,80,128]{4,3,2,1,0:T(8,128)(2,1)} %get-tuple-element.101), channel_id=1, source_target_pairs={{1,2},{2,1},{3,4},{4,3},{5,6},{6,5},{7,8},{8,7},{9,10},{10,9},{11,... | collective-permute-start | bytes 1966088 | tf_op jit(solution)/shard_map/cond/branch_1_fun/ppermute | solution.py:386
  32.3 1.9 %collective-permute-start.14 = (bf16[8,2,2,80,128]{4,3,2,1,0:T(8,128)(2,1)}, bf16[8,2,2,80,128]{4,3,2,1,0:T(8,128)(2,1)S(1)}, u32[]{:S(2)}, u32[]{:S(2)}) collective-permute-start(bf16[8,2,2,80,128]{4,3,2,1,0:T(8,128)(2,1)} %get-tuple-element.101), channel_id=1, source_target_pairs={{0,1},{1,0},{2,3},{3,2},{4,5},{5,4},{6,7},{7,6},{8,9},{9,8},{10,11... | collective-permute-start | bytes 1966088 | tf_op jit(solution)/shard_map/cond/branch_1_fun/ppermute | solution.py:386
  34.2 2.4 %collective-permute-start.18 = (bf16[8,2,80,128]{3,2,1,0:T(8,128)(2,1)S(1)}, bf16[8,2,80,128]{3,2,1,0:T(8,128)(2,1)S(1)}, u32[]{:S(2)}, u32[]{:S(2)}) collective-permute-start(bf16[8,2,80,128]{3,2,1,0:T(8,128)(2,1)S(1)} %collective-permute-done.16.prev_ref), channel_id=1, source_target_pairs={{0,1},{1,0},{2,3},{3,2},{4,5},{5,4},{6,7},{7,6},{8,9},{9,8},{10,11... | collective-permute-start | bytes 983048 | tf_op jit(solution)/shard_map/cond/branch_1_fun/ppermute | solution.py:386
  36.7 8.4 %collective-permute-done.17.next_ref = bf16[8,2,80,128]{3,2,1,0:T(8,128)(2,1)S(1)} collective-permute-done((bf16[8,2,80,128]{3,2,1,0:T(8,128)(2,1)}, bf16[8,2,80,128]{3,2,1,0:T(8,128)(2,1)S(1)}, u32[]{:S(2)}, u32[]{:S(2)}) %collective-permute-start.17) | collective-permute-done | bytes 327712 | tf_op jit(solution)/shard_map/cond/branch_1_fun/ppermute | solution.py:386
  45.1 1.9 %collective-permute-start.19 = (bf16[8,2,80,128]{3,2,1,0:T(8,128)(2,1)S(1)}, bf16[8,2,80,128]{3,2,1,0:T(8,128)(2,1)S(1)}, u32[]{:S(2)}, u32[]{:S(2)}) collective-permute-start(bf16[8,2,80,128]{3,2,1,0:T(8,128)(2,1)S(1)} %collective-permute-done.17.next_ref), channel_id=1, source_target_pairs={{0,1},{1,0},{2,3},{3,2},{4,5},{5,4},{6,7},{7,6},{8,9},{9,8},{10,11... | collective-permute-start | bytes 983048 | tf_op jit(solution)/shard_map/cond/branch_1_fun/ppermute | solution.py:386
  47.0 1.6 %collective-permute-done.19.chip_next_ref = bf16[8,2,80,128]{3,2,1,0:T(8,128)(2,1)S(1)} collective-permute-done((bf16[8,2,80,128]{3,2,1,0:T(8,128)(2,1)S(1)}, bf16[8,2,80,128]{3,2,1,0:T(8,128)(2,1)S(1)}, u32[]{:S(2)}, u32[]{:S(2)}) %collective-permute-start.19) | collective-permute-done | bytes 327712 | tf_op jit(solution)/shard_map/cond/branch_1_fun/ppermute | solution.py:386
  48.6 1.0 collective-permute-done.15.off_ref
  49.6 0.8 copy-done.15
  50.5 0.2 copy-done.16
  50.7 14.2 %attend.5 = (bf16[2,80,1536]{2,1,0:T(8,128)(2,1)}, f32[12,2,2,80,128]{4,3,2,1,0:T(8,128)}, bf16[14,2,2,80,128]{4,3,2,1,0:T(8,128)(2,1)}, bf16[14,2,2,80,128]{4,3...) custom-call(s32[12,3]{1,0:T(8,128)} %copy.60.window_ref, ...), custom_call_target="tpu_custom_call" | custom-call | tf_op jit(solution)/shard_map/cond/branch_1_fun/attend/pallas_call | solution.py:276
  64.9 2.1 %collective-permute-start.20 = (bf16[14,2,2,80,128]{4,3,2,1,0:T(8,128)(2,1)}, bf16[14,2,2,80,128]{4,3,2,1,0:T(8,128)(2,1)S(1)}, u32[]{:S(2)}, u32[]{:S(2)}) collective-permute-start(bf16[14,2,2,80,128]{4,3,2,1,0:T(8,128)(2,1)} %get-tuple-element.109), channel_id=1, source_target_pairs={{0,1},{1,0},{2,3},{3,2},{4,5},{5,4},{6,7},{7,6},{8,9},{9,8},{10,11... | collective-permute-start | bytes 3440648 | tf_op jit(solution)/shard_map/cond/branch_1_fun/ppermute | solution.py:386
  67.0 5.8 %collective-permute-start.21 = (bf16[14,2,2,80,128]{4,3,2,1,0:T(8,128)(2,1)}, bf16[14,2,2,80,128]{4,3,2,1,0:T(8,128)(2,1)S(1)}, u32[]{:S(2)}, u32[]{:S(2)}) collective-permute-start(bf16[14,2,2,80,128]{4,3,2,1,0:T(8,128)(2,1)} %get-tuple-element.110), channel_id=1, source_target_pairs={{1,2},{2,1},{3,4},{4,3},{5,6},{6,5},{7,8},{8,7},{9,10},{10,9},{11,... | collective-permute-start | bytes 3440648 | tf_op jit(solution)/shard_map/cond/branch_1_fun/ppermute | solution.py:386
  72.8 0.8 reshape.81
  73.8 36.7 %all_to_all.50 = f32[64,1,4]{2,1,0:T(1,128)S(1)} all-to-all(f32[64,1,4]{2,1,0:T(1,128)S(1)} %copy.51), channel_id=1, replica_groups=mesh['tm'=8,'height'=64] {'height'}, dimensions={0} | all-to-all | bytes 2048 | tf_op jit(solution)/shard_map/cond/branch_1_fun/all_to_all | solution.py:401
  110.7 1.0 copy-done.7
  111.7 0.4 copy-done.8
  112.1 3.2 %add_corner_terms.5 = (bf16[8,2,80,128]{3,2,1,0:T(8,128)(2,1)}, bf16[8,2,80,128]{3,2,1,0:T(8,128)(2,1)}) custom-call(s32[12,3]{1,0:T(8,128)} %copy.60.window_ref, s32[5,12]{1,0:T(8,128)} %get-tuple-element.94.slots_ref, f32[8,2,80,128]{3,2,1,0:T(8,128)} %get-tuple-element.114.prev_ref, f32[8,2,80,128]{3,2,1,0:T(8,128)} %get-tuple-element.115.next_ref, ...), custom_call_target="tpu_custom_call" | custom-call | tf_op jit(solution)/shard_map/cond/branch_1_fun/add_corner_terms/pallas_call | solution.py:324
  115.3 2.3 %collective-permute-start.22 = (bf16[8,2,80,128]{3,2,1,0:T(8,128)(2,1)}, bf16[8,2,80,128]{3,2,1,0:T(8,128)(2,1)S(1)}, u32[]{:S(2)}, u32[]{:S(2)}) collective-permute-start(bf16[8,2,80,128]{3,2,1,0:T(8,128)(2,1)} %get-tuple-element.116), channel_id=1, source_target_pairs={{0,64},{1,65},{2,66},{3,67},{4,68},{5,69},{6,70},{7,71},{8,72},{9,... | collective-permute-start | bytes 983048 | tf_op jit(solution)/shard_map/cond/branch_1_fun/ppermute | solution.py:386
  117.7 3.8 %collective-permute-start.23 = (bf16[8,2,80,128]{3,2,1,0:T(8,128)(2,1)}, bf16[8,2,80,128]{3,2,1,0:T(8,128)(2,1)S(1)}, u32[]{:S(2)}, u32[]{:S(2)}) collective-permute-start(bf16[8,2,80,128]{3,2,1,0:T(8,128)(2,1)} %get-tuple-element.117), channel_id=1, source_target_pairs={{64,0},{65,1},{66,2},{67,3},{68,4},{69,5},{70,6},{71,7},{72,8},{73... | collective-permute-start | bytes 983048 | tf_op jit(solution)/shard_map/cond/branch_1_fun/ppermute | solution.py:386
  121.5 13.5 %all_to_all.51 = f32[8,1,4]{2,1,0:T(1,128)S(1)} all-to-all(f32[8,1,4]{2,1,0:T(1,128)S(1)} %broadcast_in_dim.21), channel_id=1, replica_groups=mesh['tm'=8,'height'=64] {'tm'}, dimensions={0} | all-to-all | bytes 256 | tf_op jit(solution)/shard_map/cond/branch_1_fun/all_to_all | solution.py:406
  135.1 0.7 copy-done.39
  135.8 0.1 copy-done.40
  135.9 4.4 %finish_keys.5 = (bf16[2,80,1536]{2,1,0:T(8,128)(2,1)}, bf16[2,80,1536]{2,1,0:T(8,128)(2,1)}) custom-call(s32[12,3]{1,0:T(8,128)} %copy.60.window_ref, s32[5,12]{1,0:T(8,128)} %get-tuple-element.94.slots_ref, bf16[2,80,1536]{2,1,0:T(8,128)(2,1)S(1)} %copy-done.1, f32[12,2,2,80,128]{4,3,2,1,0:T(8,128)} %get-tuple-element.108.own_ref, ...), custom_call_target="tpu_custom_call" | custom-call | tf_op jit(solution)/shard_map/cond/branch_1_fun/finish_keys/pallas_call | solution.py:364
  140.3 0.6 copy-done.55
  (38 shorter events, 0.5 us)
Async XLA Ops:
  13.6 18.6 %collective-permute-start.12 = (bf16[6,2,80,128]{3,2,1,0:T(8,128)(2,1)}, bf16[6,2,80,128]{3,2,1,0:T(8,128)(2,1)S(1)}, u32[]{:S(2)}, u32[]{:S(2)}) collective-permute-start(bf16[6,2,80,128]{3,2,1,0:T(8,128)(2,1)} %get-tuple-element.99), channel_id=1, source_target_pairs={{1,66},{2,65},{3,68},{4,67},{5,70},{6,69},{7,72},{8,71},{9,74},{10... | collective-permute-start | bytes 737288 | tf_op jit(solution)/shard_map/cond/branch_1_fun/ppermute | solution.py:386
  18.8 13.4 %collective-permute-start.13 = (bf16[6,2,80,128]{3,2,1,0:T(8,128)(2,1)}, bf16[6,2,80,128]{3,2,1,0:T(8,128)(2,1)S(1)}, u32[]{:S(2)}, u32[]{:S(2)}) collective-permute-start(bf16[6,2,80,128]{3,2,1,0:T(8,128)(2,1)} %get-tuple-element.100), channel_id=1, source_target_pairs={{65,2},{66,1},{67,4},{68,3},{69,6},{70,5},{71,8},{72,7},{73,10},{7... | collective-permute-start | bytes 737288 | tf_op jit(solution)/shard_map/cond/branch_1_fun/ppermute | solution.py:386
  21.3 12.9 %collective-permute-start.16 = (bf16[8,2,80,128]{3,2,1,0:T(8,128)(2,1)}, bf16[8,2,80,128]{3,2,1,0:T(8,128)(2,1)S(1)}, u32[]{:S(2)}, u32[]{:S(2)}) collective-permute-start(bf16[8,2,80,128]{3,2,1,0:T(8,128)(2,1)} %get-tuple-element.102), channel_id=1, source_target_pairs={{0,64},{1,65},{2,66},{3,67},{4,68},{5,69},{6,70},{7,71},{8,72},{9,... | collective-permute-start | bytes 983048 | tf_op jit(solution)/shard_map/cond/branch_1_fun/ppermute | solution.py:386
  23.5 21.6 %collective-permute-start.17 = (bf16[8,2,80,128]{3,2,1,0:T(8,128)(2,1)}, bf16[8,2,80,128]{3,2,1,0:T(8,128)(2,1)S(1)}, u32[]{:S(2)}, u32[]{:S(2)}) collective-permute-start(bf16[8,2,80,128]{3,2,1,0:T(8,128)(2,1)} %get-tuple-element.103), channel_id=1, source_target_pairs={{64,0},{65,1},{66,2},{67,3},{68,4},{69,5},{70,6},{71,7},{72,8},{73... | collective-permute-start | bytes 983048 | tf_op jit(solution)/shard_map/cond/branch_1_fun/ppermute | solution.py:386
  27.5 22.1 %collective-permute-start.15 = (bf16[8,2,2,80,128]{4,3,2,1,0:T(8,128)(2,1)}, bf16[8,2,2,80,128]{4,3,2,1,0:T(8,128)(2,1)S(1)}, u32[]{:S(2)}, u32[]{:S(2)}) collective-permute-start(bf16[8,2,2,80,128]{4,3,2,1,0:T(8,128)(2,1)} %get-tuple-element.101), channel_id=1, source_target_pairs={{1,2},{2,1},{3,4},{4,3},{5,6},{6,5},{7,8},{8,7},{9,10},{10,9},{11,... | collective-permute-start | bytes 1966088 | tf_op jit(solution)/shard_map/cond/branch_1_fun/ppermute | solution.py:386
  32.3 17.3 %copy-start.41 = (bf16[6,2,80,128]{3,2,1,0:T(8,128)(2,1)}, bf16[6,2,80,128]{3,2,1,0:T(8,128)(2,1)S(1)}, u32[]{:S(2)}) copy-start(bf16[6,2,80,128]{3,2,1,0:T(8,128)(2,1)S(1)} %collective-permute-done.12.off_prev_ref) | copy-start | bytes 737284 | tf_op jit(solution)/shard_map/cond
  32.3 17.3 %copy-start.42 = (bf16[6,2,80,128]{3,2,1,0:T(8,128)(2,1)}, bf16[6,2,80,128]{3,2,1,0:T(8,128)(2,1)S(1)}, u32[]{:S(2)}) copy-start(bf16[6,2,80,128]{3,2,1,0:T(8,128)(2,1)S(1)} %collective-permute-done.13.off_next_ref) | copy-start | bytes 737284 | tf_op jit(solution)/shard_map/cond
  32.3 17.3 %collective-permute-start.14 = (bf16[8,2,2,80,128]{4,3,2,1,0:T(8,128)(2,1)}, bf16[8,2,2,80,128]{4,3,2,1,0:T(8,128)(2,1)S(1)}, u32[]{:S(2)}, u32[]{:S(2)}) collective-permute-start(bf16[8,2,2,80,128]{4,3,2,1,0:T(8,128)(2,1)} %get-tuple-element.101), channel_id=1, source_target_pairs={{0,1},{1,0},{2,3},{3,2},{4,5},{5,4},{6,7},{7,6},{8,9},{9,8},{10,11... | collective-permute-start | bytes 1966088 | tf_op jit(solution)/shard_map/cond/branch_1_fun/ppermute | solution.py:386
  34.2 15.4 %copy-start.35 = (bf16[8,2,80,128]{3,2,1,0:T(8,128)(2,1)}, bf16[8,2,80,128]{3,2,1,0:T(8,128)(2,1)S(1)}, u32[]{:S(2)}) copy-start(bf16[8,2,80,128]{3,2,1,0:T(8,128)(2,1)S(1)} %collective-permute-done.16.prev_ref) | copy-start | bytes 983044 | tf_op jit(solution)/shard_map/cond
  34.2 12.8 %collective-permute-start.18 = (bf16[8,2,80,128]{3,2,1,0:T(8,128)(2,1)S(1)}, bf16[8,2,80,128]{3,2,1,0:T(8,128)(2,1)S(1)}, u32[]{:S(2)}, u32[]{:S(2)}) collective-permute-start(bf16[8,2,80,128]{3,2,1,0:T(8,128)(2,1)S(1)} %collective-permute-done.16.prev_ref), channel_id=1, source_target_pairs={{0,1},{1,0},{2,3},{3,2},{4,5},{5,4},{6,7},{7,6},{8,9},{9,8},{10,11... | collective-permute-start | bytes 983048 | tf_op jit(solution)/shard_map/cond/branch_1_fun/ppermute | solution.py:386
  45.1 4.5 %copy-start.36 = (bf16[8,2,80,128]{3,2,1,0:T(8,128)(2,1)}, bf16[8,2,80,128]{3,2,1,0:T(8,128)(2,1)S(1)}, u32[]{:S(2)}) copy-start(bf16[8,2,80,128]{3,2,1,0:T(8,128)(2,1)S(1)} %collective-permute-done.17.next_ref) | copy-start | bytes 983044 | tf_op jit(solution)/shard_map/cond
  45.1 3.5 %collective-permute-start.19 = (bf16[8,2,80,128]{3,2,1,0:T(8,128)(2,1)S(1)}, bf16[8,2,80,128]{3,2,1,0:T(8,128)(2,1)S(1)}, u32[]{:S(2)}, u32[]{:S(2)}) collective-permute-start(bf16[8,2,80,128]{3,2,1,0:T(8,128)(2,1)S(1)} %collective-permute-done.17.next_ref), channel_id=1, source_target_pairs={{0,1},{1,0},{2,3},{3,2},{4,5},{5,4},{6,7},{7,6},{8,9},{9,8},{10,11... | collective-permute-start | bytes 983048 | tf_op jit(solution)/shard_map/cond/branch_1_fun/ppermute | solution.py:386
  47.0 2.6 %copy-start.37 = (bf16[8,2,80,128]{3,2,1,0:T(8,128)(2,1)}, bf16[8,2,80,128]{3,2,1,0:T(8,128)(2,1)S(1)}, u32[]{:S(2)}) copy-start(bf16[8,2,80,128]{3,2,1,0:T(8,128)(2,1)S(1)} %collective-permute-done.18.chip_prev_ref) | copy-start | bytes 983044 | tf_op jit(solution)/shard_map/cond
  48.6 1.0 copy-start.38
  49.6 0.9 copy-start.15
  49.6 1.1 copy-start.16
  64.9 71.0 %copy-start.1 = (bf16[2,80,1536]{2,1,0:T(8,128)(2,1)S(1)}, bf16[2,80,1536]{2,1,0:T(8,128)(2,1)}, u32[]{:S(2)}) copy-start(bf16[2,80,1536]{2,1,0:T(8,128)(2,1)} %get-tuple-element.91.key_ref) | copy-start | bytes 1474564 | tf_op jit(solution)/shard_map/cond
  64.9 71.0 %copy-start.52 = (f32[1,128]{1,0:T(1,128)S(1)}, f32[1,128]{1,0:T(1,128)}, u32[]{:S(2)}) copy-start(f32[1,128]{1,0:T(1,128)} %get-tuple-element.93.gain_ref.k_gain_ref) | copy-start | bytes 1540 | tf_op jit(solution)/shard_map/cond
  64.9 45.7 %collective-permute-start.20 = (bf16[14,2,2,80,128]{4,3,2,1,0:T(8,128)(2,1)}, bf16[14,2,2,80,128]{4,3,2,1,0:T(8,128)(2,1)S(1)}, u32[]{:S(2)}, u32[]{:S(2)}) collective-permute-start(bf16[14,2,2,80,128]{4,3,2,1,0:T(8,128)(2,1)} %get-tuple-element.109), channel_id=1, source_target_pairs={{0,1},{1,0},{2,3},{3,2},{4,5},{5,4},{6,7},{7,6},{8,9},{9,8},{10,11... | collective-permute-start | bytes 3440648 | tf_op jit(solution)/shard_map/cond/branch_1_fun/ppermute | solution.py:386
  67.0 43.6 %collective-permute-start.21 = (bf16[14,2,2,80,128]{4,3,2,1,0:T(8,128)(2,1)}, bf16[14,2,2,80,128]{4,3,2,1,0:T(8,128)(2,1)S(1)}, u32[]{:S(2)}, u32[]{:S(2)}) collective-permute-start(bf16[14,2,2,80,128]{4,3,2,1,0:T(8,128)(2,1)} %get-tuple-element.110), channel_id=1, source_target_pairs={{1,2},{2,1},{3,4},{4,3},{5,6},{6,5},{7,8},{8,7},{9,10},{10,9},{11,... | collective-permute-start | bytes 3440648 | tf_op jit(solution)/shard_map/cond/branch_1_fun/ppermute | solution.py:386
  110.6 1.1 copy-start.7
  110.6 1.4 %copy-start.8 = (bf16[14,2,2,80,128]{4,3,2,1,0:T(8,128)(2,1)}, bf16[14,2,2,80,128]{4,3,2,1,0:T(8,128)(2,1)S(1)}, u32[]{:S(2)}) copy-start(bf16[14,2,2,80,128]{4,3,2,1,0:T(8,128)(2,1)S(1)} %collective-permute-done.21.off_ref) | copy-start | bytes 3440644 | tf_op jit(solution)/shard_map/cond
  115.3 19.8 %collective-permute-start.22 = (bf16[8,2,80,128]{3,2,1,0:T(8,128)(2,1)}, bf16[8,2,80,128]{3,2,1,0:T(8,128)(2,1)S(1)}, u32[]{:S(2)}, u32[]{:S(2)}) collective-permute-start(bf16[8,2,80,128]{3,2,1,0:T(8,128)(2,1)} %get-tuple-element.116), channel_id=1, source_target_pairs={{0,64},{1,65},{2,66},{3,67},{4,68},{5,69},{6,70},{7,71},{8,72},{9,... | collective-permute-start | bytes 983048 | tf_op jit(solution)/shard_map/cond/branch_1_fun/ppermute | solution.py:386
  117.7 17.4 %collective-permute-start.23 = (bf16[8,2,80,128]{3,2,1,0:T(8,128)(2,1)}, bf16[8,2,80,128]{3,2,1,0:T(8,128)(2,1)S(1)}, u32[]{:S(2)}, u32[]{:S(2)}) collective-permute-start(bf16[8,2,80,128]{3,2,1,0:T(8,128)(2,1)} %get-tuple-element.117), channel_id=1, source_target_pairs={{64,0},{65,1},{66,2},{67,3},{68,4},{69,5},{70,6},{71,7},{72,8},{73... | collective-permute-start | bytes 983048 | tf_op jit(solution)/shard_map/cond/branch_1_fun/ppermute | solution.py:386
  135.1 0.7 copy-start.39
  135.1 0.8 copy-start.40
  140.3 0.6 copy-start.55
where the time goes:
time: 142 us; the launch traced here: 141 us
  blocking collectives  50.2 us (35%)
  starting transfers between devices  38.8 us (27%)
  Pallas kernels  26.2 us (18%)
  waiting for transfers between devices  11 us (8%)
  between operations  6.48 us (5%)
  local copies, waits for them, and re-layouts  6.36 us (4%)
  other arithmetic  1.54 us (1%)
    ppermute x12, starting transfers between devices, move(): return lax.ppermute(block, BOTH, route)  38.8 us
    all_to_all x1, blocking collectives, sum_over_rows(): lax.all_to_all(pieces, 'height', 0, 0, tiled=True).sum(0, keepdims=True)  36.7 us
    pallas_call x1, Pallas kernels, attend(): pl.pallas_call(attend_kernel, in_specs=[whole(pltpu.SMEM)] * 2 + [whole()...  14.2 us
    all_to_all x1, blocking collectives, sum_over_frames(): lax.all_to_all(copies, 'tm', 0, 0, tiled=True).sum(0)  13.5 us
    ppermute x12, waiting for transfers between devices, move(): return lax.ppermute(block, BOTH, route)  11 us
    pallas_call x1, Pallas kernels, finish(): pl.pallas_call(finish_kernel, in_specs=[whole(pltpu.SMEM)] * 2 + [whole()...  4.37 us
    pallas_call x1, Pallas kernels, pack(): pl.pallas_call(pack_kernel, in_specs=[whole(pltpu.SMEM)] + [whole()] * 3,...  4.32 us
    cond x28, local copies, waits for them, and re-layouts  3.36 us
  transfers between devices with their start and end apart: 12, of which 3 were waited for; matrix products, arithmetic and copies ran while one was open for 1% of the time, Pallas kernels for 0%

commit v1 on v0

--- a/solution.py
+++ b/solution.py
@@ -49,6 +49,16 @@
     heads = channels // LANES
     edges = ((first_ref, corner_first_ref), (last_ref, corner_last_ref))
 
+    def one_norm(g, carry):
+        lanes = head_lanes(g)
+        for f in range(frames):
+            full_rows = key_ref[f, :, lanes].astype(jnp.float32)
+            own_ref[f, 0, :, lanes] = (full_rows * rms_inverse(full_rows) * gain_row).astype(jnp.bfloat16)
+            own_ref[f, 1, :, lanes] = value_ref[f, :, lanes]
+        return carry
+
+    lax.fori_loop(0, heads, one_norm, 0, unroll=4)
+
     def one_head(g, counts):
         lanes = head_lanes(g)
         row_on, frame_on = window_ref[g, 1], window_ref[g, 0]
@@ -57,32 +67,20 @@
         for kind in range(3):
             slots_ref[kind, g] = slots[kind]
         slots_ref[3, jnp.where(row_on * frame_on == 1, slots[2], heads - 1 - (g - counts[2]))] = g
-        pairs = []
-        for f in range(frames):
-            full_rows = key_ref[f, :, lanes].astype(jnp.float32)
-            pairs.append(
-                ((full_rows * rms_inverse(full_rows) * gain_row).astype(jnp.bfloat16), value_ref[f, :, lanes])
-            )
-            for c in range(2):
-                own_ref[f, c, :, lanes] = pairs[f][c]
 
         @pl.when(row_on == 1)
         def _():
+            row_ref[slots[0]] = own_ref[:, :, :, lanes]
+
+        @pl.when(frame_on == 1)
+        def _():
             for f in range(frames):
-                for c in range(2):
-                    row_ref[slots[0], f, c] = pairs[f][c]
-
-        @pl.when(frame_on == 1)
+                edges[f][0][slots[1]] = own_ref[f, :, :, lanes]
+
+        @pl.when(row_on * frame_on == 1)
         def _():
             for f in range(frames):
-                for c in range(2):
-                    edges[f][0][slots[1], c] = pairs[f][c]
-
-        @pl.when(row_on * frame_on == 1)
-        def _():
-            for f in range(frames):
-                for c in range(2):
-                    edges[f][1][slots[2], c] = pairs[f][c]
+                edges[f][1][slots[2]] = own_ref[f, :, :, lanes]
 
         return counts
 

time: 142 us -> 140 us (0.986)
  the two profiles are of different devices: /device:TPU:3 before, /device:TPU:5 now
where the time goes in v1:
time: 140 us
  blocking collectives  50.5 us (36%)
  starting transfers between devices  38.8 us (28%)
  Pallas kernels  25.6 us (18%)
  waiting for transfers between devices  10.8 us (8%)
  between operations  6.48 us (5%)
  local copies, waits for them, and re-layouts  6.36 us (5%)
  other arithmetic  1.54 us (1%)
    ppermute x12, starting transfers between devices, move(): return lax.ppermute(block, BOTH, route)  38.8 us
    all_to_all x1, blocking collectives, sum_over_rows(): lax.all_to_all(pieces, 'height', 0, 0, tiled=True).sum(0, keepdims=True)  37 us
    pallas_call x1, Pallas kernels, attend(): pl.pallas_call(attend_kernel, in_specs=[whole(pltpu.SMEM)] * 2 + [whole()...  14.2 us
    all_to_all x1, blocking collectives, sum_over_frames(): lax.all_to_all(copies, 'tm', 0, 0, tiled=True).sum(0)  13.5 us
    ppermute x12, waiting for transfers between devices, move(): return lax.ppermute(block, BOTH, route)  10.8 us
    pallas_call x1, Pallas kernels, finish(): pl.pallas_call(finish_kernel, in_specs=[whole(pltpu.SMEM)] * 2 + [whole()...  4.37 us
    pallas_call x1, Pallas kernels, pack(): pl.pallas_call(pack_kernel, in_specs=[whole(pltpu.SMEM)] + [whole()] * 3,...  3.83 us
    cond x28, local copies, waits for them, and re-layouts  3.36 us
  transfers between devices with their start and end apart: 12, of which 3 were waited for; matrix products, arithmetic and copies ran while one was open for 1% of the time, Pallas kernels for 0%

profile of v1, /device:TPU:5, one launch (start us, length us, event | category | flops | bytes accessed | tf_op | source)
XLA Modules:
  0.0 140.3 jit_solution(9169857783835423573)
XLA Ops:
  0.6 1.4 %multiply_reduce_fusion = (s32[]{:T(128)}, s32[]{:T(128)}, s32[]{:T(128)}) fusion(s32[12,3]{0,1:T(4,128)} %param.17), kind=kLoop, calls=%fused_computation | loop fusion | flops 45 | bytes 108 | tf_op jit(solution)/shard_map/reduce_sum | solution.py:444
  7.9 131.9 %conditional.1 = (bf16[2,80,1536]{2,1,0:T(8,128)(2,1)}, bf16[2,80,1536]{2,1,0:T(8,128)(2,1)}, bf16[2,80,1536]{2,1,0:T(8,128)(2,1)}, f32[2,2]{1,0:T(2,128)S(1)}) conditional(s32[]{:T(128)} %clamp.3, (s32[12,3]{0,1:T(4,128)}, bf16[2,80,1536]{2,1,0:T(8,128)(2,1)}, bf16[2,80,1536]{2,1,0:T(8,128)(2,1)}, ...), branch_computations={%region_3.0_spmd, %region_6.0_spmd, %region_9.0_spmd, %region_12.0... | conditional | flops 280 | bytes 72757984 | solution.py:451
  7.9 1.4 copy.60.window_ref
  9.3 3.8 %pack_keys_values.5 = (s32[5,12]{1,0:T(8,128)}, bf16[2,2,80,1536]{3,2,1,0:T(8,128)(2,1)}, bf16[8,2,2,80,128]{4,3,2,1,0:T(8,128)(2,1)}, bf16[8,2,80,128]{3,2,1,0:...) custom-call(s32[12,3]{1,0:T(8,128)} %copy.60.window_ref, ...), custom_call_target="tpu_custom_call" | custom-call | tf_op jit(solution)/shard_map/cond/branch_1_fun/pack_keys_values/pallas_call | solution.py:98
  13.1 5.2 %collective-permute-start.12 = (bf16[6,2,80,128]{3,2,1,0:T(8,128)(2,1)}, bf16[6,2,80,128]{3,2,1,0:T(8,128)(2,1)S(1)}, u32[]{:S(2)}, u32[]{:S(2)}) collective-permute-start(bf16[6,2,80,128]{3,2,1,0:T(8,128)(2,1)} %get-tuple-element.99), channel_id=1, source_target_pairs={{1,66},{2,65},{3,68},{4,67},{5,70},{6,69},{7,72},{8,71},{9,74},{10... | collective-permute-start | bytes 737288 | tf_op jit(solution)/shard_map/cond/branch_1_fun/ppermute | solution.py:384
  18.3 2.5 %collective-permute-start.13 = (bf16[6,2,80,128]{3,2,1,0:T(8,128)(2,1)}, bf16[6,2,80,128]{3,2,1,0:T(8,128)(2,1)S(1)}, u32[]{:S(2)}, u32[]{:S(2)}) collective-permute-start(bf16[6,2,80,128]{3,2,1,0:T(8,128)(2,1)} %get-tuple-element.100), channel_id=1, source_target_pairs={{65,2},{66,1},{67,4},{68,3},{69,6},{70,5},{71,8},{72,7},{73,10},{7... | collective-permute-start | bytes 737288 | tf_op jit(solution)/shard_map/cond/branch_1_fun/ppermute | solution.py:384
  20.8 1.9 %collective-permute-start.16 = (bf16[8,2,80,128]{3,2,1,0:T(8,128)(2,1)}, bf16[8,2,80,128]{3,2,1,0:T(8,128)(2,1)S(1)}, u32[]{:S(2)}, u32[]{:S(2)}) collective-permute-start(bf16[8,2,80,128]{3,2,1,0:T(8,128)(2,1)} %get-tuple-element.102), channel_id=1, source_target_pairs={{0,64},{1,65},{2,66},{3,67},{4,68},{5,69},{6,70},{7,71},{8,72},{9,... | collective-permute-start | bytes 983048 | tf_op jit(solution)/shard_map/cond/branch_1_fun/ppermute | solution.py:384
  22.7 4.3 %collective-permute-start.17 = (bf16[8,2,80,128]{3,2,1,0:T(8,128)(2,1)}, bf16[8,2,80,128]{3,2,1,0:T(8,128)(2,1)S(1)}, u32[]{:S(2)}, u32[]{:S(2)}) collective-permute-start(bf16[8,2,80,128]{3,2,1,0:T(8,128)(2,1)} %get-tuple-element.103), channel_id=1, source_target_pairs={{64,0},{65,1},{66,2},{67,3},{68,4},{69,5},{70,6},{71,7},{72,8},{73... | collective-permute-start | bytes 983048 | tf_op jit(solution)/shard_map/cond/branch_1_fun/ppermute | solution.py:384
  27.0 4.7 %collective-permute-start.15 = (bf16[8,2,2,80,128]{4,3,2,1,0:T(8,128)(2,1)}, bf16[8,2,2,80,128]{4,3,2,1,0:T(8,128)(2,1)S(1)}, u32[]{:S(2)}, u32[]{:S(2)}) collective-permute-start(bf16[8,2,2,80,128]{4,3,2,1,0:T(8,128)(2,1)} %get-tuple-element.101), channel_id=1, source_target_pairs={{1,2},{2,1},{3,4},{4,3},{5,6},{6,5},{7,8},{8,7},{9,10},{10,9},{11,... | collective-permute-start | bytes 1966088 | tf_op jit(solution)/shard_map/cond/branch_1_fun/ppermute | solution.py:384
  31.8 1.9 %collective-permute-start.14 = (bf16[8,2,2,80,128]{4,3,2,1,0:T(8,128)(2,1)}, bf16[8,2,2,80,128]{4,3,2,1,0:T(8,128)(2,1)S(1)}, u32[]{:S(2)}, u32[]{:S(2)}) collective-permute-start(bf16[8,2,2,80,128]{4,3,2,1,0:T(8,128)(2,1)} %get-tuple-element.101), channel_id=1, source_target_pairs={{0,1},{1,0},{2,3},{3,2},{4,5},{5,4},{6,7},{7,6},{8,9},{9,8},{10,11... | collective-permute-start | bytes 1966088 | tf_op jit(solution)/shard_map/cond/branch_1_fun/ppermute | solution.py:384
  33.7 2.4 %collective-permute-start.18 = (bf16[8,2,80,128]{3,2,1,0:T(8,128)(2,1)S(1)}, bf16[8,2,80,128]{3,2,1,0:T(8,128)(2,1)S(1)}, u32[]{:S(2)}, u32[]{:S(2)}) collective-permute-start(bf16[8,2,80,128]{3,2,1,0:T(8,128)(2,1)S(1)} %collective-permute-done.16.prev_ref), channel_id=1, source_target_pairs={{0,1},{1,0},{2,3},{3,2},{4,5},{5,4},{6,7},{7,6},{8,9},{9,8},{10,11... | collective-permute-start | bytes 983048 | tf_op jit(solution)/shard_map/cond/branch_1_fun/ppermute | solution.py:384
  36.2 8.4 %collective-permute-done.17.next_ref = bf16[8,2,80,128]{3,2,1,0:T(8,128)(2,1)S(1)} collective-permute-done((bf16[8,2,80,128]{3,2,1,0:T(8,128)(2,1)}, bf16[8,2,80,128]{3,2,1,0:T(8,128)(2,1)S(1)}, u32[]{:S(2)}, u32[]{:S(2)}) %collective-permute-start.17) | collective-permute-done | bytes 327712 | tf_op jit(solution)/shard_map/cond/branch_1_fun/ppermute | solution.py:384
  44.6 1.9 %collective-permute-start.19 = (bf16[8,2,80,128]{3,2,1,0:T(8,128)(2,1)S(1)}, bf16[8,2,80,128]{3,2,1,0:T(8,128)(2,1)S(1)}, u32[]{:S(2)}, u32[]{:S(2)}) collective-permute-start(bf16[8,2,80,128]{3,2,1,0:T(8,128)(2,1)S(1)} %collective-permute-done.17.next_ref), channel_id=1, source_target_pairs={{0,1},{1,0},{2,3},{3,2},{4,5},{5,4},{6,7},{7,6},{8,9},{9,8},{10,11... | collective-permute-start | bytes 983048 | tf_op jit(solution)/shard_map/cond/branch_1_fun/ppermute | solution.py:384
  46.5 1.6 %collective-permute-done.19.chip_next_ref = bf16[8,2,80,128]{3,2,1,0:T(8,128)(2,1)S(1)} collective-permute-done((bf16[8,2,80,128]{3,2,1,0:T(8,128)(2,1)S(1)}, bf16[8,2,80,128]{3,2,1,0:T(8,128)(2,1)S(1)}, u32[]{:S(2)}, u32[]{:S(2)}) %collective-permute-start.19) | collective-permute-done | bytes 327712 | tf_op jit(solution)/shard_map/cond/branch_1_fun/ppermute | solution.py:384
  48.1 0.7 collective-permute-done.15.off_ref
  48.9 0.8 copy-done.15
  49.8 0.2 copy-done.16
  50.0 14.2 %attend.5 = (bf16[2,80,1536]{2,1,0:T(8,128)(2,1)}, f32[12,2,2,80,128]{4,3,2,1,0:T(8,128)}, bf16[14,2,2,80,128]{4,3,2,1,0:T(8,128)(2,1)}, bf16[14,2,2,80,128]{4,3...) custom-call(s32[12,3]{1,0:T(8,128)} %copy.60.window_ref, ...), custom_call_target="tpu_custom_call" | custom-call | tf_op jit(solution)/shard_map/cond/branch_1_fun/attend/pallas_call | solution.py:274
  64.2 2.1 %collective-permute-start.20 = (bf16[14,2,2,80,128]{4,3,2,1,0:T(8,128)(2,1)}, bf16[14,2,2,80,128]{4,3,2,1,0:T(8,128)(2,1)S(1)}, u32[]{:S(2)}, u32[]{:S(2)}) collective-permute-start(bf16[14,2,2,80,128]{4,3,2,1,0:T(8,128)(2,1)} %get-tuple-element.109), channel_id=1, source_target_pairs={{0,1},{1,0},{2,3},{3,2},{4,5},{5,4},{6,7},{7,6},{8,9},{9,8},{10,11... | collective-permute-start | bytes 3440648 | tf_op jit(solution)/shard_map/cond/branch_1_fun/ppermute | solution.py:384
  66.3 5.7 %collective-permute-start.21 = (bf16[14,2,2,80,128]{4,3,2,1,0:T(8,128)(2,1)}, bf16[14,2,2,80,128]{4,3,2,1,0:T(8,128)(2,1)S(1)}, u32[]{:S(2)}, u32[]{:S(2)}) collective-permute-start(bf16[14,2,2,80,128]{4,3,2,1,0:T(8,128)(2,1)} %get-tuple-element.110), channel_id=1, source_target_pairs={{1,2},{2,1},{3,4},{4,3},{5,6},{6,5},{7,8},{8,7},{9,10},{10,9},{11,... | collective-permute-start | bytes 3440648 | tf_op jit(solution)/shard_map/cond/branch_1_fun/ppermute | solution.py:384
  72.0 0.8 reshape.81
  73.0 37.0 %all_to_all.50 = f32[64,1,4]{2,1,0:T(1,128)S(1)} all-to-all(f32[64,1,4]{2,1,0:T(1,128)S(1)} %copy.51), channel_id=1, replica_groups=mesh['tm'=8,'height'=64] {'height'}, dimensions={0} | all-to-all | bytes 2048 | tf_op jit(solution)/shard_map/cond/branch_1_fun/all_to_all | solution.py:399
  110.1 1.0 copy-done.7
  111.2 0.4 copy-done.8
  111.5 3.2 %add_corner_terms.5 = (bf16[8,2,80,128]{3,2,1,0:T(8,128)(2,1)}, bf16[8,2,80,128]{3,2,1,0:T(8,128)(2,1)}) custom-call(s32[12,3]{1,0:T(8,128)} %copy.60.window_ref, s32[5,12]{1,0:T(8,128)} %get-tuple-element.94.slots_ref, f32[8,2,80,128]{3,2,1,0:T(8,128)} %get-tuple-element.114.prev_ref, f32[8,2,80,128]{3,2,1,0:T(8,128)} %get-tuple-element.115.next_ref, ...), custom_call_target="tpu_custom_call" | custom-call | tf_op jit(solution)/shard_map/cond/branch_1_fun/add_corner_terms/pallas_call | solution.py:322
  114.8 2.3 %collective-permute-start.22 = (bf16[8,2,80,128]{3,2,1,0:T(8,128)(2,1)}, bf16[8,2,80,128]{3,2,1,0:T(8,128)(2,1)S(1)}, u32[]{:S(2)}, u32[]{:S(2)}) collective-permute-start(bf16[8,2,80,128]{3,2,1,0:T(8,128)(2,1)} %get-tuple-element.116), channel_id=1, source_target_pairs={{0,64},{1,65},{2,66},{3,67},{4,68},{5,69},{6,70},{7,71},{8,72},{9,... | collective-permute-start | bytes 983048 | tf_op jit(solution)/shard_map/cond/branch_1_fun/ppermute | solution.py:384
  117.1 3.8 %collective-permute-start.23 = (bf16[8,2,80,128]{3,2,1,0:T(8,128)(2,1)}, bf16[8,2,80,128]{3,2,1,0:T(8,128)(2,1)S(1)}, u32[]{:S(2)}, u32[]{:S(2)}) collective-permute-start(bf16[8,2,80,128]{3,2,1,0:T(8,128)(2,1)} %get-tuple-element.117), channel_id=1, source_target_pairs={{64,0},{65,1},{66,2},{67,3},{68,4},{69,5},{70,6},{71,7},{72,8},{73... | collective-permute-start | bytes 983048 | tf_op jit(solution)/shard_map/cond/branch_1_fun/ppermute | solution.py:384
  121.0 13.5 %all_to_all.51 = f32[8,1,4]{2,1,0:T(1,128)S(1)} all-to-all(f32[8,1,4]{2,1,0:T(1,128)S(1)} %broadcast_in_dim.21), channel_id=1, replica_groups=mesh['tm'=8,'height'=64] {'tm'}, dimensions={0} | all-to-all | bytes 256 | tf_op jit(solution)/shard_map/cond/branch_1_fun/all_to_all | solution.py:404
  134.6 0.7 copy-done.39
  135.3 0.1 copy-done.40
  135.4 4.4 %finish_keys.5 = (bf16[2,80,1536]{2,1,0:T(8,128)(2,1)}, bf16[2,80,1536]{2,1,0:T(8,128)(2,1)}) custom-call(s32[12,3]{1,0:T(8,128)} %copy.60.window_ref, s32[5,12]{1,0:T(8,128)} %get-tuple-element.94.slots_ref, bf16[2,80,1536]{2,1,0:T(8,128)(2,1)S(1)} %copy-done.1, f32[12,2,2,80,128]{4,3,2,1,0:T(8,128)} %get-tuple-element.108.own_ref, ...), custom_call_target="tpu_custom_call" | custom-call | tf_op jit(solution)/shard_map/cond/branch_1_fun/finish_keys/pallas_call | solution.py:362
  139.8 0.6 copy-done.55
  (38 shorter events, 0.5 us)
Async XLA Ops:
  13.1 18.6 %collective-permute-start.12 = (bf16[6,2,80,128]{3,2,1,0:T(8,128)(2,1)}, bf16[6,2,80,128]{3,2,1,0:T(8,128)(2,1)S(1)}, u32[]{:S(2)}, u32[]{:S(2)}) collective-permute-start(bf16[6,2,80,128]{3,2,1,0:T(8,128)(2,1)} %get-tuple-element.99), channel_id=1, source_target_pairs={{1,66},{2,65},{3,68},{4,67},{5,70},{6,69},{7,72},{8,71},{9,74},{10... | collective-permute-start | bytes 737288 | tf_op jit(solution)/shard_map/cond/branch_1_fun/ppermute | solution.py:384
  18.3 13.4 %collective-permute-start.13 = (bf16[6,2,80,128]{3,2,1,0:T(8,128)(2,1)}, bf16[6,2,80,128]{3,2,1,0:T(8,128)(2,1)S(1)}, u32[]{:S(2)}, u32[]{:S(2)}) collective-permute-start(bf16[6,2,80,128]{3,2,1,0:T(8,128)(2,1)} %get-tuple-element.100), channel_id=1, source_target_pairs={{65,2},{66,1},{67,4},{68,3},{69,6},{70,5},{71,8},{72,7},{73,10},{7... | collective-permute-start | bytes 737288 | tf_op jit(solution)/shard_map/cond/branch_1_fun/ppermute | solution.py:384
  20.8 12.9 %collective-permute-start.16 = (bf16[8,2,80,128]{3,2,1,0:T(8,128)(2,1)}, bf16[8,2,80,128]{3,2,1,0:T(8,128)(2,1)S(1)}, u32[]{:S(2)}, u32[]{:S(2)}) collective-permute-start(bf16[8,2,80,128]{3,2,1,0:T(8,128)(2,1)} %get-tuple-element.102), channel_id=1, source_target_pairs={{0,64},{1,65},{2,66},{3,67},{4,68},{5,69},{6,70},{7,71},{8,72},{9,... | collective-permute-start | bytes 983048 | tf_op jit(solution)/shard_map/cond/branch_1_fun/ppermute | solution.py:384
  22.7 21.9 %collective-permute-start.17 = (bf16[8,2,80,128]{3,2,1,0:T(8,128)(2,1)}, bf16[8,2,80,128]{3,2,1,0:T(8,128)(2,1)S(1)}, u32[]{:S(2)}, u32[]{:S(2)}) collective-permute-start(bf16[8,2,80,128]{3,2,1,0:T(8,128)(2,1)} %get-tuple-element.103), channel_id=1, source_target_pairs={{64,0},{65,1},{66,2},{67,3},{68,4},{69,5},{70,6},{71,7},{72,8},{73... | collective-permute-start | bytes 983048 | tf_op jit(solution)/shard_map/cond/branch_1_fun/ppermute | solution.py:384
  27.0 21.8 %collective-permute-start.15 = (bf16[8,2,2,80,128]{4,3,2,1,0:T(8,128)(2,1)}, bf16[8,2,2,80,128]{4,3,2,1,0:T(8,128)(2,1)S(1)}, u32[]{:S(2)}, u32[]{:S(2)}) collective-permute-start(bf16[8,2,2,80,128]{4,3,2,1,0:T(8,128)(2,1)} %get-tuple-element.101), channel_id=1, source_target_pairs={{1,2},{2,1},{3,4},{4,3},{5,6},{6,5},{7,8},{8,7},{9,10},{10,9},{11,... | collective-permute-start | bytes 1966088 | tf_op jit(solution)/shard_map/cond/branch_1_fun/ppermute | solution.py:384
  31.8 17.1 %copy-start.41 = (bf16[6,2,80,128]{3,2,1,0:T(8,128)(2,1)}, bf16[6,2,80,128]{3,2,1,0:T(8,128)(2,1)S(1)}, u32[]{:S(2)}) copy-start(bf16[6,2,80,128]{3,2,1,0:T(8,128)(2,1)S(1)} %collective-permute-done.12.off_prev_ref) | copy-start | bytes 737284 | tf_op jit(solution)/shard_map/cond
  31.8 17.1 %copy-start.42 = (bf16[6,2,80,128]{3,2,1,0:T(8,128)(2,1)}, bf16[6,2,80,128]{3,2,1,0:T(8,128)(2,1)S(1)}, u32[]{:S(2)}) copy-start(bf16[6,2,80,128]{3,2,1,0:T(8,128)(2,1)S(1)} %collective-permute-done.13.off_next_ref) | copy-start | bytes 737284 | tf_op jit(solution)/shard_map/cond
  31.8 17.1 %collective-permute-start.14 = (bf16[8,2,2,80,128]{4,3,2,1,0:T(8,128)(2,1)}, bf16[8,2,2,80,128]{4,3,2,1,0:T(8,128)(2,1)S(1)}, u32[]{:S(2)}, u32[]{:S(2)}) collective-permute-start(bf16[8,2,2,80,128]{4,3,2,1,0:T(8,128)(2,1)} %get-tuple-element.101), channel_id=1, source_target_pairs={{0,1},{1,0},{2,3},{3,2},{4,5},{5,4},{6,7},{7,6},{8,9},{9,8},{10,11... | collective-permute-start | bytes 1966088 | tf_op jit(solution)/shard_map/cond/branch_1_fun/ppermute | solution.py:384
  33.7 15.1 %copy-start.35 = (bf16[8,2,80,128]{3,2,1,0:T(8,128)(2,1)}, bf16[8,2,80,128]{3,2,1,0:T(8,128)(2,1)S(1)}, u32[]{:S(2)}) copy-start(bf16[8,2,80,128]{3,2,1,0:T(8,128)(2,1)S(1)} %collective-permute-done.16.prev_ref) | copy-start | bytes 983044 | tf_op jit(solution)/shard_map/cond
  33.7 12.8 %collective-permute-start.18 = (bf16[8,2,80,128]{3,2,1,0:T(8,128)(2,1)S(1)}, bf16[8,2,80,128]{3,2,1,0:T(8,128)(2,1)S(1)}, u32[]{:S(2)}, u32[]{:S(2)}) collective-permute-start(bf16[8,2,80,128]{3,2,1,0:T(8,128)(2,1)S(1)} %collective-permute-done.16.prev_ref), channel_id=1, source_target_pairs={{0,1},{1,0},{2,3},{3,2},{4,5},{5,4},{6,7},{7,6},{8,9},{9,8},{10,11... | collective-permute-start | bytes 983048 | tf_op jit(solution)/shard_map/cond/branch_1_fun/ppermute | solution.py:384
  44.6 4.3 %copy-start.36 = (bf16[8,2,80,128]{3,2,1,0:T(8,128)(2,1)}, bf16[8,2,80,128]{3,2,1,0:T(8,128)(2,1)S(1)}, u32[]{:S(2)}) copy-start(bf16[8,2,80,128]{3,2,1,0:T(8,128)(2,1)S(1)} %collective-permute-done.17.next_ref) | copy-start | bytes 983044 | tf_op jit(solution)/shard_map/cond
  44.6 3.5 %collective-permute-start.19 = (bf16[8,2,80,128]{3,2,1,0:T(8,128)(2,1)S(1)}, bf16[8,2,80,128]{3,2,1,0:T(8,128)(2,1)S(1)}, u32[]{:S(2)}, u32[]{:S(2)}) collective-permute-start(bf16[8,2,80,128]{3,2,1,0:T(8,128)(2,1)S(1)} %collective-permute-done.17.next_ref), channel_id=1, source_target_pairs={{0,1},{1,0},{2,3},{3,2},{4,5},{5,4},{6,7},{7,6},{8,9},{9,8},{10,11... | collective-permute-start | bytes 983048 | tf_op jit(solution)/shard_map/cond/branch_1_fun/ppermute | solution.py:384
  46.5 2.4 %copy-start.37 = (bf16[8,2,80,128]{3,2,1,0:T(8,128)(2,1)}, bf16[8,2,80,128]{3,2,1,0:T(8,128)(2,1)S(1)}, u32[]{:S(2)}) copy-start(bf16[8,2,80,128]{3,2,1,0:T(8,128)(2,1)S(1)} %collective-permute-done.18.chip_prev_ref) | copy-start | bytes 983044 | tf_op jit(solution)/shard_map/cond
  48.1 0.8 copy-start.38
  48.9 0.9 copy-start.15
  48.9 1.1 copy-start.16
  64.2 71.2 %copy-start.1 = (bf16[2,80,1536]{2,1,0:T(8,128)(2,1)S(1)}, bf16[2,80,1536]{2,1,0:T(8,128)(2,1)}, u32[]{:S(2)}) copy-start(bf16[2,80,1536]{2,1,0:T(8,128)(2,1)} %get-tuple-element.91.key_ref) | copy-start | bytes 1474564 | tf_op jit(solution)/shard_map/cond
  64.2 71.2 %copy-start.52 = (f32[1,128]{1,0:T(1,128)S(1)}, f32[1,128]{1,0:T(1,128)}, u32[]{:S(2)}) copy-start(f32[1,128]{1,0:T(1,128)} %get-tuple-element.93.gain_ref.k_gain_ref) | copy-start | bytes 1540 | tf_op jit(solution)/shard_map/cond
  64.2 45.9 %collective-permute-start.20 = (bf16[14,2,2,80,128]{4,3,2,1,0:T(8,128)(2,1)}, bf16[14,2,2,80,128]{4,3,2,1,0:T(8,128)(2,1)S(1)}, u32[]{:S(2)}, u32[]{:S(2)}) collective-permute-start(bf16[14,2,2,80,128]{4,3,2,1,0:T(8,128)(2,1)} %get-tuple-element.109), channel_id=1, source_target_pairs={{0,1},{1,0},{2,3},{3,2},{4,5},{5,4},{6,7},{7,6},{8,9},{9,8},{10,11... | collective-permute-start | bytes 3440648 | tf_op jit(solution)/shard_map/cond/branch_1_fun/ppermute | solution.py:384
  66.3 43.9 %collective-permute-start.21 = (bf16[14,2,2,80,128]{4,3,2,1,0:T(8,128)(2,1)}, bf16[14,2,2,80,128]{4,3,2,1,0:T(8,128)(2,1)S(1)}, u32[]{:S(2)}, u32[]{:S(2)}) collective-permute-start(bf16[14,2,2,80,128]{4,3,2,1,0:T(8,128)(2,1)} %get-tuple-element.110), channel_id=1, source_target_pairs={{1,2},{2,1},{3,4},{4,3},{5,6},{6,5},{7,8},{8,7},{9,10},{10,9},{11,... | collective-permute-start | bytes 3440648 | tf_op jit(solution)/shard_map/cond/branch_1_fun/ppermute | solution.py:384
  110.1 1.1 copy-start.7
  110.1 1.4 %copy-start.8 = (bf16[14,2,2,80,128]{4,3,2,1,0:T(8,128)(2,1)}, bf16[14,2,2,80,128]{4,3,2,1,0:T(8,128)(2,1)S(1)}, u32[]{:S(2)}) copy-start(bf16[14,2,2,80,128]{4,3,2,1,0:T(8,128)(2,1)S(1)} %collective-permute-done.21.off_ref) | copy-start | bytes 3440644 | tf_op jit(solution)/shard_map/cond
  114.8 19.8 %collective-permute-start.22 = (bf16[8,2,80,128]{3,2,1,0:T(8,128)(2,1)}, bf16[8,2,80,128]{3,2,1,0:T(8,128)(2,1)S(1)}, u32[]{:S(2)}, u32[]{:S(2)}) collective-permute-start(bf16[8,2,80,128]{3,2,1,0:T(8,128)(2,1)} %get-tuple-element.116), channel_id=1, source_target_pairs={{0,64},{1,65},{2,66},{3,67},{4,68},{5,69},{6,70},{7,71},{8,72},{9,... | collective-permute-start | bytes 983048 | tf_op jit(solution)/shard_map/cond/branch_1_fun/ppermute | solution.py:384
  117.1 17.5 %collective-permute-start.23 = (bf16[8,2,80,128]{3,2,1,0:T(8,128)(2,1)}, bf16[8,2,80,128]{3,2,1,0:T(8,128)(2,1)S(1)}, u32[]{:S(2)}, u32[]{:S(2)}) collective-permute-start(bf16[8,2,80,128]{3,2,1,0:T(8,128)(2,1)} %get-tuple-element.117), channel_id=1, source_target_pairs={{64,0},{65,1},{66,2},{67,3},{68,4},{69,5},{70,6},{71,7},{72,8},{73... | collective-permute-start | bytes 983048 | tf_op jit(solution)/shard_map/cond/branch_1_fun/ppermute | solution.py:384
  134.6 0.7 copy-start.39
  134.6 0.8 copy-start.40
  139.8 0.6 copy-start.55
